TPU v7x, 32 devices: a whole 2x2x4 slice. The times are simulated.
32 devices in a mesh: dp: 8 (over z, x), mp: 4 (over y, core).
Axes of the slice: x: 2, y: 2, z: 4, core: 2. Of those that a mesh axis runs over, the one named last changes fastest.
Arguments:
- inputs: bfloat16 [24576, 768], P(('dp', 'mp')), may hold values from -6 to 6
- cotangent: bfloat16 [24576, 768], P(('dp', 'mp')), may hold values from -6 to 6
- routes: int32 [24576, 1], P('dp'), may hold values from 0 to 7; in each aligned block of 768 rows (0 to 767, 768 to 1535, ...) at most 120 rows name the same one
- domains: int32 [24], P('dp'), may hold values from 0 to 7
- domain_counts: int32 [8], replicated, may hold values from 5 to 15
- domain_weights: float32 [8], replicated, may hold values from 0.5 to 2
- keep_mask: int32 [24], P('dp'), may hold values 0 or 1
- gain_one: float32 [768], replicated, may hold values from 0.5 to 1.5
- shift_one: float32 [768], replicated, may hold values from -1.8 to 1.8
- w_qkv: bfloat16 [768, 3, 768], P(None, None, 'mp'), may hold values from -0.21875 to 0.21875
- w_proj: bfloat16 [768, 768], P('mp'), may hold values from -0.625 to 0.625
- gain_two: float32 [768], replicated, may hold values from 0.5 to 1.5
- shift_two: float32 [768], replicated, may hold values from -1.8 to 1.8
- w_router: bfloat16 [768, 8], replicated, may hold values from -0.15625 to 0.15625
- w_in: bfloat16 [8, 768, 3072], P('dp', None, 'mp'), may hold values from -0.21875 to 0.21875
- w_out: bfloat16 [8, 3072, 768], P('dp', 'mp'), may hold values from -0.21875 to 0.21875
Outputs:
- output: bfloat16 [24576, 768], P(('dp', 'mp'))
- input_grad: bfloat16 [24576, 768], P(('dp', 'mp'))
- grad_gain_one: float32 [768], replicated
- grad_shift_one: float32 [768], replicated
- grad_w_qkv: float32 [768, 3, 768], P(None, None, 'mp')
- grad_w_proj: float32 [768, 768], P('mp')
- grad_gain_two: float32 [768], replicated
- grad_shift_two: float32 [768], replicated
- grad_router: float32 [768, 8], replicated
- grad_w_in: float32 [8, 768, 3072], P('dp', None, 'mp')
- grad_w_out: float32 [8, 3072, 768], P('dp', 'mp')
Inputs may be any that keep to these rules, and one draw needn't show every extreme that they name: `routes`: within the rows of one device (aligned blocks of 768 tokens) each expert is named by at most 120 rows, a bound that some block reaches.
All inputs are finite; a program needn't handle non-finite values. No bound on the sum of `keep_mask` on one device may be relied on, other than what follows from the above.
Results may differ from a plain program's by a relative error of at most 0.015.
Values may be sent and summed in bfloat16 or wider, within the bound.
A program may use at most 192 MiB of HBM per device.

v0:
```python
import functools

import jax
import jax.numpy as jnp
from jax import lax
from jax.experimental import pallas as pl
from jax.experimental.pallas import tpu as pltpu
from jax.sharding import PartitionSpec as P

HEAD_DIM = 64
LEN = 1024
BLOCK = 256
HALF = LEN // 2

norm_epsilon = 1e-05
count_scale = 10.0
masked_score = -1e30

f32 = jnp.float32
bf16 = jnp.bfloat16
MESH = pl.DeviceIdType.MESH
NT = (((1,), (1,)), ((), ()))
NN = (((1,), (0,)), ((), ()))
TN = (((0,), (0,)), ((), ()))


def dot(left, right, dims=NN):
    return lax.dot_general(left, right, dims, preferred_element_type=f32)


def mask_diagonal(scores, whole):
    first = lax.broadcasted_iota(jnp.int32, (BLOCK, BLOCK), 0)
    second = lax.broadcasted_iota(jnp.int32, (BLOCK, BLOCK), 1)
    last = jnp.where(first <= second, scores[whole * BLOCK :], masked_score)
    if not whole:
        return last
    return jnp.concatenate([scores[: whole * BLOCK], last], axis=0)


def remote(src, dst, send, recv, device):
    return pltpu.make_async_remote_copy(
        src_ref=src, dst_ref=dst, send_sem=send, recv_sem=recv, device_id=device, device_id_type=MESH
    )


def greet(devices):
    barrier = pltpu.get_barrier_semaphore()
    for device in devices:
        pl.semaphore_signal(barrier, inc=1, device_id=device, device_id_type=MESH)
    pl.semaphore_wait(barrier, len(devices))


def normalise(values):
    centre = values - jnp.mean(values, axis=-1, keepdims=True)
    inverse = lax.rsqrt(jnp.mean(centre * centre, axis=-1, keepdims=True) + norm_epsilon)
    return centre * inverse, inverse


def norm_pull(d_normed, scaled, inverse, gain):
    d_scaled = d_normed * gain
    return inverse * (
        d_scaled
        - jnp.mean(d_scaled, axis=-1, keepdims=True)
        - scaled * jnp.mean(d_scaled * scaled, axis=-1, keepdims=True)
    )


PAIRS = 3
PAIR = 2 * HEAD_DIM
STRIP = 256


def pick_sequence(positions, loss):
    domains, counts, weights, keep = loss
    value = jnp.zeros(positions.shape, f32)
    for index in range(domains.shape[0]):
        domain = domains[index]
        weight = jnp.full(positions.shape, keep[index].astype(f32) * weights[domain], f32)
        factor = weight * count_scale / jnp.full(positions.shape, counts[domain].astype(f32), f32)
        value = jnp.where(positions >= index * LEN, factor, value)
    return value


def forward_kernel(
    experts, slots, cap,
    domains_ref, counts_ref, weights_ref, keep_ref, x_ref, cot_ref, routes_ref, gain_one_ref, shift_one_ref, gain_two_ref, shift_two_ref,
    w_ref, proj_ref, w_in_ref,
    normed_out, qkv_out, ext_out, mixed_out, log_out, heads_out, proj_out, hidden_out, rows_out, cot_out,
    placing_t_out, w_in_far_out,
    normed, qkv, ext, mixed, logs, heads, proj, hidden, rows, placing, placing_t, cot_send, mixed_far, normed_two,
    keys, values,
    w_sems, pass_sems, proj_sems, w_in_sems, normed_sems, ext_sems, mixed_sems, row_send, row_recv, local_sems,
    save_sems,
):
    me, mp = lax.axis_index("dp"), lax.axis_index("mp")
    chip, core = mp // 2, mp % 2
    tok, width = x_ref.shape
    part = proj_ref.shape[0]
    total = experts * slots
    beside = {"mp": mp + 1 - 2 * core}
    across = {"mp": (mp + 2) % 4}
    side = me % 2
    partner = {"dp": me + 1 - 2 * side}
    second = chip == 1
    others = [(me + k) % experts for k in range(1, experts)]
    greet([{"dp": other} for other in others] + [beside, across])

    own_part = pl.ds(pl.multiple_of(chip * part, 16), part)
    other_part = pl.ds(pl.multiple_of((1 - chip) * part, 16), part)
    half = pl.ds(pl.multiple_of(side * (width // 2), 128), width // 2)

    def w_copy(index):
        if index == 3:
            source, target = proj_ref.at[:, half], proj.at[0, own_part, half]
        else:
            source, target = w_ref.at[index, :, half], heads.at[index, own_part, half]
        return remote(source, target, w_sems.at[0, index], w_sems.at[1, index], across)

    def w_pass(index):
        block = proj.at[0, other_part, half] if index == 3 else heads.at[index, other_part, half]
        return remote(block, block, pass_sems.at[0, index], pass_sems.at[1, index], partner)

    proj_pass = remote(proj.at[0], proj.at[1], proj_sems.at[0], proj_sems.at[1], beside)
    w_in_copy = remote(w_in_ref, w_in_far_out, w_in_sems.at[0], w_in_sems.at[1], across)
    for index in range(4):
        w_copy(index).start()
    w_local = pltpu.make_async_copy(w_ref, heads.at[:, own_part], local_sems.at[0])
    proj_local = pltpu.make_async_copy(proj_ref, proj.at[0, own_part], local_sems.at[1])
    w_local.start()
    proj_local.start()

    mine = pl.multiple_of(core * tok, tok)

    def first_norm(step, carry):
        at = pl.ds(pl.multiple_of(step * STRIP, STRIP), STRIP)
        scaled, _ = normalise(x_ref[at].astype(f32))
        normed[pl.ds(pl.multiple_of(HALF + mine + step * STRIP, STRIP), STRIP)] = (
            scaled * gain_one_ref[...][None, :] + shift_one_ref[...][None, :]
        ).astype(bf16)
        return carry

    lax.fori_loop(0, tok // STRIP, first_norm, 0)
    own_normed = normed.at[pl.ds(pl.multiple_of(HALF + mine, STRIP), tok)]
    normed_copy = remote(own_normed, own_normed, normed_sems.at[0], normed_sems.at[1], beside)
    normed_copy.start()

    wide = max(16, experts)
    own_routes = routes_ref[:, pl.ds(pl.multiple_of(mp * tok, tok), tok)]
    picked = own_routes == lax.broadcasted_iota(jnp.int32, (wide, tok), 0)
    earlier = lax.broadcasted_iota(jnp.int32, (tok, tok), 0) < lax.broadcasted_iota(jnp.int32, (tok, tok), 1)
    counts = dot(jnp.where(picked, 1.0, 0.0).astype(bf16), jnp.where(earlier, 1.0, 0.0).astype(bf16))
    rank = jnp.sum(jnp.where(picked, counts, 0.0), axis=0, keepdims=True)
    slot_of = own_routes.astype(f32) * slots + rank

    def place(step, carry):
        ids = lax.broadcasted_iota(jnp.int32, (STRIP, tok), 0) + step * STRIP
        at = pl.ds(pl.multiple_of(step * STRIP, STRIP), STRIP)
        placing[at] = jnp.where(ids.astype(f32) == slot_of, 1.0, 0.0).astype(bf16)
        return carry

    lax.fori_loop(0, total // STRIP, place, 0)

    positions = mp * tok + lax.broadcasted_iota(jnp.int32, (1, tok), 1)
    factors = pick_sequence(positions, (domains_ref, counts_ref, weights_ref, keep_ref))
    high = factors.astype(bf16)
    low = (factors - high.astype(f32)).astype(bf16)
    which = lax.broadcasted_iota(jnp.int32, (16, tok), 0)
    both = jnp.where(which == 0, high, jnp.where(which == 1, low, bf16(0)))
    spread = dot(both, placing[...], NT)

    def place_cot(step, carry):
        at = pl.ds(pl.multiple_of(step * STRIP, STRIP), STRIP)
        cot_send[at] = dot(placing[at], cot_ref[...]).astype(bf16)
        return carry

    lax.fori_loop(0, total // STRIP, place_cot, 0)
    spare = lax.broadcasted_iota(jnp.int32, (16, slots), 0) == cap - (slots - 16)
    for expert in range(experts):
        at = slice((expert + 1) * slots - 16, (expert + 1) * slots)
        here = slice(expert * slots, (expert + 1) * slots)
        for term, column in ((0, 0), (1, width // 2)):
            cot_send[at, column : column + slots] = jnp.where(
                spare, spread[term : term + 1, here], cot_send[at, column : column + slots].astype(f32)
            ).astype(bf16)

    def chunk(index):
        return pl.ds(pl.multiple_of(index * slots, 16), slots)

    def row_copy(target, source):
        return remote(
            cot_send.at[chunk(target)], cot_out.at[chunk(source)],
            row_send.at[target], row_recv.at[source], {"dp": target},
        )

    own_rows = pltpu.make_async_copy(cot_send.at[chunk(me)], cot_out.at[chunk(me)], local_sems.at[2])
    own_rows.start()
    same_side = [(me + k) % experts for k in range(2, experts, 2)]
    for other in same_side:
        row_copy(other, me).start()

    def turn(step, carry):
        at = pl.ds(pl.multiple_of(step * STRIP, STRIP), STRIP)
        placing_t[:, at] = placing[at].T
        return carry

    lax.fori_loop(0, total // STRIP, turn, 0)

    saves = []

    def save(source, target):
        copy = pltpu.make_async_copy(source, target, save_sems.at[len(saves)])
        copy.start()
        saves.append(copy)

    save(placing_t, placing_t_out)

    def pair_of(step):
        return (1 - chip) * step + chip * (PAIRS - 1 - step)

    def column(offset, pair):
        return pl.ds(pl.multiple_of((offset * PAIRS + pair) * PAIR, PAIR), PAIR)

    def project(step):
        pair = pair_of(step)
        weights = jnp.concatenate([heads[index, column(0, pair)] for index in range(3)])

        def strip_of(strip, carry):
            at = pl.ds(pl.multiple_of(strip * 512, 512), 512)
            value = dot(normed[pl.ds(pl.multiple_of(HALF + strip * 512, 512), 512)], weights, NT).astype(bf16)
            for index in range(3):
                qkv[at, column(index, pair)] = value[:, index * PAIR : (index + 1) * PAIR]
            return carry

        lax.fori_loop(0, 2 * tok // 512, strip_of, 0)

    lane = lax.broadcasted_iota(jnp.int32, (1, PAIR), 1)
    row = lax.broadcasted_iota(jnp.int32, (PAIR, 1), 0)

    def attend_blocks(pair, blocks):
        items = [(first, whole, head) for first, whole in blocks for head in range(2)]

        def start(first, whole, head):
            span = (whole + 1) * BLOCK
            near = pl.ds(pl.multiple_of(first + HALF - whole * BLOCK, BLOCK), span)
            queries = qkv[pl.ds(first, BLOCK), column(0, pair)] * bf16(0.125)
            own = jnp.where((lane // HEAD_DIM) == head, queries, bf16(0))
            return near, dot(keys[near], own, NT)

        waiting = start(*items[0])
        parts = []
        for index, (first, whole, head) in enumerate(items):
            near, scores = waiting
            if index + 1 < len(items):
                waiting = start(*items[index + 1])
            scores = mask_diagonal(scores, whole)
            largest = jnp.max(scores, axis=0, keepdims=True)
            expo = jnp.exp(scores - largest)
            summed = jnp.sum(expo, axis=0, keepdims=True)
            parts.append(dot(values[:, near], expo.astype(bf16)) / summed)
            at = pl.ds(first, BLOCK)
            logs[pair, head : head + 1, at] = largest + jnp.log(summed)
            if head:
                mixed[at, column(0, pair)] = jnp.where(row < HEAD_DIM, parts[-2], parts[-1]).T.astype(bf16)

    quarter = HALF // 2
    ext_rows = pl.ds(pl.multiple_of(core * quarter, quarter), quarter)
    ext_copy = remote(
        normed.at[pl.ds(pl.multiple_of(2 * tok + core * quarter, quarter), quarter)], normed.at[ext_rows],
        ext_sems.at[0, 0], ext_sems.at[1, 0], across,
    )
    ext_pass = remote(normed.at[ext_rows], normed.at[ext_rows], ext_sems.at[0, 1], ext_sems.at[1, 1], beside)
    w_local.wait()
    normed_copy.wait_recv()

    @pl.when(chip == 0)
    def _():
        ext_copy.start()

    w_in_copy.start()
    project(0)
    for index in range(4):
        w_copy(index).wait_recv()
        w_pass(index).start()

    def attention(step, carry):
        pair = pair_of(step)

        @pl.when(step == 1)
        def _():
            for index in range(3):
                w_pass(index).wait_recv()
            for other in [(me + k) % experts for k in range(1, experts, 2)]:
                row_copy(other, me).start()
            project(1)
            project(2)

        keys[HALF:] = qkv[:, column(1, pair)]
        values[:, HALF:] = qkv[:, column(2, pair)].T
        attend_blocks(pair, [(pl.multiple_of((2 * chip + whole) * BLOCK, BLOCK), whole) for whole in range(4)])

        @pl.when(chip == 0)
        def _():
            attend_blocks(pair, [(4 * BLOCK, 0), (5 * BLOCK, 1)])

        return carry

    lax.fori_loop(0, PAIRS, attention, 0)
    save(qkv, qkv_out)
    save(heads, heads_out)
    proj_local.wait()
    w_pass(3).wait_recv()
    proj_pass.start()
    save(proj.at[0], proj_out)

    @pl.when(second)
    def _():
        ext_copy.wait_recv()
        ext_pass.start()
        ext_pass.wait_recv()
        for index in range(2):
            ext[:, index * PAIRS * PAIR : (index + 1) * PAIRS * PAIR] = dot(
                normed[0:HALF], heads[1 + index], NT
            ).astype(bf16)

        def late(pair, carry):
            keys[0:HALF] = ext[:, column(0, pair)]
            keys[HALF : 2 * HALF] = qkv[0:HALF, column(1, pair)]
            values[:, 0:HALF] = ext[:, column(1, pair)].T
            values[:, HALF : 2 * HALF] = qkv[0:HALF, column(2, pair)].T
            attend_blocks(pair, [(0, 2), (BLOCK, 3)])
            return carry

        lax.fori_loop(0, PAIRS, late, 0)

    @pl.when(chip == 0)
    def _():
        ext_copy.wait_send()
        ext[...] = jnp.zeros_like(ext)
        normed[0:HALF] = jnp.zeros((HALF, width), bf16)

    @pl.when(second)
    def _():
        ext_pass.wait_send()

    save(normed, normed_out)
    save(ext, ext_out)
    save(mixed, mixed_out)
    save(logs, log_out)
    mixed_copy = remote(
        mixed.at[pl.ds(pl.multiple_of((1 - core) * tok, tok), tok)], mixed_far,
        mixed_sems.at[0], mixed_sems.at[1], beside,
    )
    mixed_copy.start()
    proj_pass.wait_recv()
    mixed_copy.wait_recv()

    def second_norm(step, carry):
        at = pl.ds(pl.multiple_of(step * STRIP, STRIP), STRIP)
        value = x_ref[at].astype(f32) + (
            dot(mixed[pl.ds(pl.multiple_of(mine + step * STRIP, STRIP), STRIP)], proj[0])
            + dot(mixed_far[at], proj[1])
        )
        hidden[at] = value
        scaled, _ = normalise(value)
        normed_two[at] = (scaled * gain_two_ref[...][None, :] + shift_two_ref[...][None, :]).astype(bf16)
        return carry

    lax.fori_loop(0, tok // STRIP, second_norm, 0)
    save(hidden, hidden_out)

    def place_rows(step, carry):
        at = pl.ds(pl.multiple_of(step * STRIP, STRIP), STRIP)
        rows[at] = dot(placing[at], normed_two[...]).astype(bf16)
        return carry

    lax.fori_loop(0, total // STRIP, place_rows, 0)
    save(rows, rows_out)
    own_rows.wait()
    for other in others:
        row_copy(me, other).wait_recv()
        row_copy(other, me).wait_send()
    for index in range(4):
        w_copy(index).wait_send()
        w_pass(index).wait_send()
    for copy in (proj_pass, normed_copy, mixed_copy):
        copy.wait_send()
    for copy in saves:
        copy.wait()
    w_in_copy.wait()


def run_forward(
    loss, x, cotangent, routes, gain_one, shift_one, gain_two, shift_two, w_heads, w_proj, w_in, experts, cap, slots
):
    tok, width = x.shape
    rows = 2 * tok
    total = experts * slots
    part = w_proj.shape[0]
    anyspace, vmem = pl.BlockSpec(memory_space=pl.ANY), pl.BlockSpec(memory_space=pltpu.VMEM)
    smem = pl.BlockSpec(memory_space=pltpu.SMEM)
    dma = pltpu.SemaphoreType.DMA
    kept = [
        ((HALF + rows, width), bf16),
        ((rows, 3 * PAIRS * PAIR), bf16),
        ((HALF, 2 * PAIRS * PAIR), bf16),
        ((rows, PAIRS * PAIR), bf16),
        ((PAIRS, 8, rows), f32),
        ((3, 2 * part, width), bf16),
    ]
    late = [((tok, width), f32), ((total, width), bf16)]
    return pl.pallas_call(
        functools.partial(forward_kernel, experts, slots, cap),
        in_specs=[smem] * 4 + [vmem] * 7 + [anyspace] * 3,
        out_specs=[anyspace] * 12,
        out_shape=[
            jax.ShapeDtypeStruct(*item)
            for item in kept
            + [((2 * part, width), bf16)]
            + late
            + [((total, width), bf16), ((tok, total), bf16), (w_in.shape, bf16)]
        ],
        scratch_shapes=[pltpu.VMEM(*item) for item in kept + [((2, 2 * part, width), bf16)] + late]
        + [
            pltpu.VMEM((total, tok), bf16),
            pltpu.VMEM((tok, total), bf16),
            pltpu.VMEM((total, width), bf16),
            pltpu.VMEM((tok, PAIRS * PAIR), bf16),
            pltpu.VMEM((tok, width), bf16),
            pltpu.VMEM((HALF + rows, PAIR), bf16),
            pltpu.VMEM((PAIR, HALF + rows), bf16),
            dma((2, 4)), dma((2, 4)), dma((2,)), dma((2,)), dma((2,)), dma((2, 2)), dma((2,)),
            dma((experts,)), dma((experts,)), dma((3,)), dma((10,)),
        ],
        compiler_params=pltpu.CompilerParams(
            collective_id=4, has_side_effects=True, vmem_limit_bytes=56 * 2**20
        ),
        cost_estimate=pl.CostEstimate(flops=30 * 10**9, bytes_accessed=30 * 10**6, transcendentals=8 * 10**6),
        name="forward",
    )(*loss, x, cotangent, routes, gain_one, shift_one, gain_two, shift_two, w_heads, w_proj, w_in)


def backward_kernel(
    experts, slots,
    domains_ref, counts_ref, weights_ref, keep_ref,
    hidden_ref, gain_one_ref, gain_two_ref, placing_ref, d_returned_ref, router_ref,
    cot_any, result_ref, there_in_ref, there_out_ref, mixed_any, proj_any, qkv_any, ext_any, log_any, normed_any, heads_any, x_any,
    output_ref, input_grad_ref, total_ref, small_ref, far_in_ref, far_out_ref,
    mixed_ref, proj_ref, qkv_ref, ext_ref, log_ref, normed_ref, heads_ref, x_ref, saved,
    summed, returned, d_hidden, d_branch, d_mixed, keys, values, d_keys, d_values, d_qkv, d_ext,
    grads_own, grads_send, grads_recv, d_norm, norm_recv, ext_recv,
    held, half_recv, piece_recv, small, first_slots, second_slots, last_slots,
    row_send, row_recv, branch_sems, norm_sems, ext_sems, far_sems, grad_sems,
    half_sems, piece_sems, gather_sems, back_sems, small_sems, load_sems, local_sems,
):
    me, mp = lax.axis_index("dp"), lax.axis_index("mp")
    chip, core = mp // 2, mp % 2
    tok, width = hidden_ref.shape
    rows = 2 * tok
    part = grads_own.shape[1]
    all_heads = PAIRS * PAIR
    beside = {"mp": mp + 1 - 2 * core}
    across = {"mp": (mp + 2) % 4}
    second = chip == 1
    others = [(me + k) % experts for k in range(1, experts)]
    diagonal = {"mp": 3 - mp}
    greet([{"dp": other} for other in others] + [beside, across, diagonal])

    def chunk(index):
        return pl.ds(pl.multiple_of(index * slots, 16), slots)

    def row_copy(target, source):
        return remote(
            result_ref.at[chunk(target)], returned.at[chunk(source)],
            row_send.at[target], row_recv.at[source], {"dp": target},
        )

    cot_copy = pltpu.make_async_copy(cot_any, grads_send, local_sems.at[1])
    cot_copy.start()
    loads = [
        pltpu.make_async_copy(source, target, load_sems.at[index])
        for index, (source, target) in enumerate(
            (
                (mixed_any, mixed_ref), (proj_any, proj_ref), (qkv_any, qkv_ref), (ext_any, ext_ref),
                (log_any, log_ref), (normed_any, normed_ref), (heads_any, heads_ref), (x_any, x_ref),
            )
        )
    ]
    for load in loads:
        load.start()
    far_half = there_in_ref.shape[0] // 2
    far_copies = [
        remote(
            there_out_ref.at[pl.ds(far_half, far_half)], far_out_ref, far_sems.at[0, 0], far_sems.at[1, 0], across
        )
    ] + [
        remote(
            there_in_ref.at[pl.ds(index * far_half, far_half)], far_in_ref.at[pl.ds(index * far_half, far_half)],
            far_sems.at[0, 1 + index], far_sems.at[1, 1 + index], across,
        )
        for index in range(2)
    ]
    far_copies[0].start()
    far_copies[1].start()
    own_rows = pltpu.make_async_copy(result_ref.at[chunk(me)], returned.at[chunk(me)], local_sems.at[0])
    own_rows.start()
    for other in others:
        row_copy(other, me).start()

    cot_copy.wait()
    small[...] = jnp.zeros_like(small)
    mine = pl.multiple_of(core * tok, tok)

    def second_norm(step, carry):
        at = pl.ds(pl.multiple_of(step * STRIP, STRIP), STRIP)
        scaled, inverse = normalise(hidden_ref[at])
        d_normed = dot(placing_ref[at], d_returned_ref[...])
        small[2:3] += jnp.sum(d_normed * scaled, axis=0, keepdims=True)
        small[3:4] += jnp.sum(d_normed, axis=0, keepdims=True)
        positions = mp * tok + step * STRIP + lax.broadcasted_iota(jnp.int32, (STRIP, 1), 0)
        total = grads_send[at].astype(f32) * pick_sequence(
            positions, (domains_ref, counts_ref, weights_ref, keep_ref)
        ) + norm_pull(
            d_normed, scaled, inverse, gain_two_ref[...][None, :]
        )
        d_hidden[at] = total
        d_branch[pl.ds(pl.multiple_of(mine + step * STRIP, STRIP), STRIP)] = total.astype(bf16)
        return carry

    lax.fori_loop(0, tok // STRIP, second_norm, 0)
    own_branch = d_branch.at[pl.ds(mine, tok)]
    branch_copy = remote(own_branch, own_branch, branch_sems.at[0], branch_sems.at[1], beside)
    branch_copy.start()

    for load in loads[:2]:
        load.wait()

    def push_branch(base):
        def push(step, carry):
            at = pl.ds(pl.multiple_of(base + step * STRIP, STRIP), STRIP)
            d_mixed[at] = dot(d_branch[at], proj_ref[...], NT).astype(bf16)
            return carry

        lax.fori_loop(0, tok // STRIP, push, 0)

    push_branch(mine)
    branch_copy.wait()
    push_branch((1 - core) * tok)

    side, line = me % 2, me // 2
    lines = experts // 2
    partner = {"dp": me + 1 - 2 * side}
    mates = [(line + k) % lines for k in range(1, lines)]
    piece_rows = held.shape[1] // lines
    own_columns = pl.ds(pl.multiple_of(side * (width // 2), 128), width // 2)
    other_columns = pl.ds(pl.multiple_of((1 - side) * (width // 2), 128), width // 2)

    def piece(index):
        return pl.ds(pl.multiple_of(index * piece_rows, 16), piece_rows)

    def sent(index):
        return slice(index * part, (index + 1) * part)

    def grad_copy(index):
        return remote(
            grads_send.at[sent(index)], grads_recv.at[index], grad_sems.at[0, index], grad_sems.at[1, index], across
        )

    def half_copy(index):
        return remote(
            held.at[index, :, other_columns], half_recv.at[index],
            half_sems.at[0, index], half_sems.at[1, index], partner,
        )

    def piece_copy(index, target, source):
        return remote(
            held.at[index, piece(target), own_columns], piece_recv.at[index, source],
            piece_sems.at[0, index, target], piece_sems.at[1, index, source], {"dp": 2 * target + side},
        )

    def gather_copy(index, target, source):
        block = total_ref.at[index, piece(source), own_columns]
        return remote(
            block, block,
            gather_sems.at[0, index, target], gather_sems.at[1, index, source], {"dp": 2 * target + side},
        )

    def back_copy(index):
        block = total_ref.at[index, :, own_columns]
        return remote(block, block, back_sems.at[0, index], back_sems.at[1, index], partner)

    def product(left, right, first):
        def block(step, carry):
            at = pl.ds(pl.multiple_of(first + step * PAIR, PAIR), PAIR)
            summed[pl.ds(pl.multiple_of(step * PAIR, PAIR), PAIR)] = dot(left[:, at], right[...], TN)
            return carry

        lax.fori_loop(0, PAIRS, block, 0)

    def send_grad(index):
        grads_own[index] = summed[pl.ds(pl.multiple_of(chip * part, 16), part)]
        grads_send[sent(index)] = summed[pl.ds(pl.multiple_of((1 - chip) * part, 16), part)].astype(bf16)

        grad_copy(index).start()

    chunks = held.shape[0]
    parts = 4 // chunks

    def stage_one(index):
        if index >= chunks:
            return
        for at in range(parts):
            number = index * parts + at
            grad_copy(number).wait_recv()
            held[index, at * part : (at + 1) * part] = (
                grads_own[number] + grads_recv[number].astype(f32)
            ).astype(bf16)
        if held.shape[1] > parts * part:
            held[index, parts * part :] = jnp.zeros((held.shape[1] - parts * part, width), bf16)
        half_copy(index).start()

    def stage_two(index):
        if index >= chunks:
            return
        half_copy(index).wait_recv()
        held[index, :, own_columns] = (
            held[index, :, own_columns].astype(f32) + half_recv[index].astype(f32)
        ).astype(bf16)
        for mate in mates:
            piece_copy(index, mate, line).start()

    def stage_three(index):
        if index >= chunks:
            return
        value = held[index, piece(line), own_columns].astype(f32)
        for mate in mates:
            piece_copy(index, line, mate).wait_recv()
            value += piece_recv[index, mate].astype(f32)
        total_ref[index, piece(line), own_columns] = value.astype(bf16)
        for mate in mates:
            gather_copy(index, mate, line).start()

    def stage_four(index):
        if index >= chunks:
            return
        for mate in mates:
            gather_copy(index, line, mate).wait_recv()
        back_copy(index).start()

    product(mixed_ref, d_branch, 0)
    send_grad(0)

    lane = lax.broadcasted_iota(jnp.int32, (1, PAIR), 1)

    def column(offset, pair):
        return pl.ds(pl.multiple_of((offset * PAIRS + pair) * PAIR, PAIR), PAIR)

    def attend_blocks(pair, blocks):
        for first, whole in blocks:
            span = (whole + 1) * BLOCK
            start = pl.multiple_of(first + HALF - whole * BLOCK, BLOCK)
            at = pl.ds(first, BLOCK)
            queries = qkv_ref[at, column(0, pair)] * bf16(0.125)
            d_out = d_mixed[at, column(0, pair)]
            near = keys[pl.ds(start, span)]
            near_values = values[pl.ds(start, span)]
            product = (d_out.astype(f32) * mixed_ref[at, column(0, pair)].astype(f32)).T
            dq = dk = dv = 0.0
            for head in range(2):
                here = (lane // HEAD_DIM) == head
                own = jnp.where(here, queries, bf16(0))
                d_own = jnp.where(here, d_out, bf16(0))
                delta = jnp.sum(product[HEAD_DIM * head : HEAD_DIM * (head + 1)], axis=0, keepdims=True)
                scores = mask_diagonal(dot(near, own, NT), whole)
                probs = jnp.exp(scores - log_ref[pair, head : head + 1, at])
                d_probs = dot(near_values, d_own, NT)
                d_scores = (probs * (d_probs - delta)).astype(bf16)
                dv = dv + dot(probs.astype(bf16), d_own)
                dk = dk + dot(d_scores, own)
                dq = dq + dot(d_scores, jnp.where(here, near, bf16(0)), TN)
            d_qkv[at, column(0, pair)] = (dq * 0.125).astype(bf16)
            d_keys[pl.ds(start, span)] += dk
            d_values[pl.ds(start, span)] += dv

    ext_part, norm_send = d_branch.at[tok : tok + HALF], d_branch.at[0:tok]
    ext_beside = remote(ext_part, ext_recv, ext_sems.at[0, 0], ext_sems.at[1, 0], beside)
    ext_across = remote(ext_part, ext_recv, ext_sems.at[0, 1], ext_sems.at[1, 1], across)
    for load in loads[2:5]:
        load.wait()

    @pl.when(second)
    def _():
        def early(pair, carry):
            keys[0:HALF] = ext_ref[:, column(0, pair)]
            keys[HALF : 2 * HALF] = qkv_ref[0:HALF, column(1, pair)]
            values[0:HALF] = ext_ref[:, column(1, pair)]
            values[HALF : 2 * HALF] = qkv_ref[0:HALF, column(2, pair)]
            d_keys[0 : 2 * HALF] = jnp.zeros((2 * HALF, PAIR), f32)
            d_values[0 : 2 * HALF] = jnp.zeros((2 * HALF, PAIR), f32)
            attend_blocks(pair, [(0, 2), (BLOCK, 3)])
            d_ext[:, column(0, pair)] = d_keys[0:HALF].astype(bf16)
            d_ext[:, column(1, pair)] = d_values[0:HALF].astype(bf16)
            saved[pair, :, 0:PAIR] = d_keys[HALF : 2 * HALF]
            saved[pair, :, PAIR:] = d_values[HALF : 2 * HALF]
            return carry

        lax.fori_loop(0, PAIRS, early, 0)

    for load in loads[5:7]:
        load.wait()

    @pl.when(second)
    def _():
        ext_part[...] = dot(d_ext[...], heads_ref[1:3].reshape(2 * all_heads, width)).astype(bf16)

    @pl.when(chip == 0)
    def _():
        d_ext[...] = jnp.zeros_like(d_ext)
        saved[...] = jnp.zeros_like(saved)

    @pl.when(mp == 2)
    def _():
        ext_beside.start()

    def attention(pair, carry):
        keys[HALF:] = qkv_ref[:, column(1, pair)]
        values[HALF:] = qkv_ref[:, column(2, pair)]
        d_keys[HALF : 2 * HALF] = saved[pair, :, 0:PAIR]
        d_keys[2 * HALF :] = jnp.zeros((rows - HALF, PAIR), f32)
        d_values[HALF : 2 * HALF] = saved[pair, :, PAIR:]
        d_values[2 * HALF :] = jnp.zeros((rows - HALF, PAIR), f32)
        attend_blocks(pair, [(pl.multiple_of((2 * chip + whole) * BLOCK, BLOCK), whole) for whole in range(4)])

        @pl.when(chip == 0)
        def _():
            attend_blocks(pair, [(4 * BLOCK, 0), (5 * BLOCK, 1)])

        @pl.when((mp == 3) & (pair == 0))
        def _():
            ext_beside.wait_recv()
            ext_part[...] = (ext_part[...].astype(f32) + ext_recv[...].astype(f32)).astype(bf16)
            ext_across.start()

        d_qkv[:, column(1, pair)] = d_keys[HALF:].astype(bf16)
        d_qkv[:, column(2, pair)] = d_values[HALF:].astype(bf16)
        return carry

    lax.fori_loop(0, PAIRS, attention, 0)

    product(d_qkv, normed_ref.at[HALF:], 0)
    send_grad(1)

    for index in (1, 2):
        product(d_qkv, normed_ref.at[HALF:], index * all_heads)

        @pl.when(second)
        def _():
            def block(step, carry):
                at = pl.ds(pl.multiple_of((index - 1) * all_heads + step * PAIR, PAIR), PAIR)
                summed[pl.ds(pl.multiple_of(step * PAIR, PAIR), PAIR)] += dot(d_ext[:, at], normed_ref[0:HALF], TN)
                return carry

            lax.fori_loop(0, PAIRS, block, 0)

        send_grad(1 + index)
    stage_one(0)

    weights = heads_ref[...].reshape(3 * all_heads, width)

    def push_norm(step, carry):
        at = pl.ds(pl.multiple_of((1 - core) * tok + step * STRIP, STRIP), STRIP)
        norm_send[pl.ds(pl.multiple_of(step * STRIP, STRIP), STRIP)] = dot(d_qkv[at], weights).astype(bf16)
        return carry

    def pull_norm(step, carry):
        at = pl.ds(pl.multiple_of(mine + step * STRIP, STRIP), STRIP)
        d_norm[pl.ds(pl.multiple_of(step * STRIP, STRIP), STRIP)] = dot(d_qkv[at], weights)
        return carry

    lax.fori_loop(0, tok // STRIP, push_norm, 0)
    norm_copy = remote(norm_send, norm_recv, norm_sems.at[0], norm_sems.at[1], beside)
    norm_copy.start()
    lax.fori_loop(0, tok // STRIP, pull_norm, 0)
    stage_two(0)
    stage_one(1)
    own_rows.wait()
    for other in others:
        row_copy(me, other).wait_recv()

    def finish(step, carry):
        at = pl.ds(pl.multiple_of(step * STRIP, STRIP), STRIP)
        output_ref[at] = (hidden_ref[at] + dot(placing_ref[at], returned[...])).astype(bf16)
        return carry

    lax.fori_loop(0, tok // STRIP, finish, 0)
    stage_three(0)
    stage_two(1)
    stage_one(2)
    norm_copy.wait_recv()
    loads[7].wait()

    @pl.when(mp == 1)
    def _():
        ext_across.wait_recv()
        d_norm[tok - HALF :] += ext_recv[...].astype(f32)

    def first_norm(step, carry):
        at = pl.ds(pl.multiple_of(step * STRIP, STRIP), STRIP)
        scaled, inverse = normalise(x_ref[at].astype(f32))
        d_normed = d_norm[at] + norm_recv[at].astype(f32)
        small[0:1] += jnp.sum(d_normed * scaled, axis=0, keepdims=True)
        small[1:2] += jnp.sum(d_normed, axis=0, keepdims=True)
        input_grad_ref[at] = (
            d_hidden[at] + norm_pull(d_normed, scaled, inverse, gain_one_ref[...][None, :])
        ).astype(bf16)
        return carry

    lax.fori_loop(0, tok // STRIP, first_norm, 0)

    small[4:5] = router_ref[...]
    rounds = [(first_slots, "dp", me, me - me % 8, 1, 8)]
    if experts > 8:
        rounds.append((second_slots, "dp", me, me % 8, 8, 8))
    rounds.append((last_slots, "mp", mp, mp - mp % 4, 1, 4))

    def small_copies(number, receiving):
        slots_of, axis, place, base, step, size = rounds[number]
        own = (place - base) // step
        copies = []
        for k in range(1, size):
            other = (own + k) % size
            source, target = (other, own) if receiving else (own, other)
            copies.append(
                remote(
                    slots_of.at[own], slots_of.at[source],
                    small_sems.at[0, number, target], small_sems.at[1, number, source],
                    {axis: base + other * step},
                )
            )
        return copies

    def small_start(number):
        for copy in small_copies(number, False):
            copy.start()

    def small_finish(number):
        for copy in small_copies(number, True):
            copy.wait_recv()
        slots_of, size = rounds[number][0], rounds[number][-1]
        value = slots_of[0]
        for index in range(1, size):
            value += slots_of[index]
        return value

    first_slots[me % 8] = small[...]
    small_start(0)
    stage_four(0)
    stage_three(1)
    stage_two(2)
    norms = small_finish(0)
    if experts > 8:
        second_slots[me // 8, 0:8] = norms
        for index in range(8):
            second_slots[me // 8, 8 + index : 9 + index] = first_slots[index, 4:5]
        small_start(1)
        norms = small_finish(1)
        for index in range(8):
            last_slots[mp % 4, 8 + 8 * index : 16 + 8 * index] = second_slots[index, 8:16]
    else:
        for index in range(8):
            last_slots[mp % 4, 8 + index : 9 + index] = first_slots[index, 4:5]
    last_slots[mp % 4, 0:8] = norms[0:8]
    small_start(len(rounds) - 1)
    far_copies[2].start()
    stage_one(3)
    stage_four(1)
    stage_three(2)
    stage_two(3)
    stage_four(2)
    stage_three(3)
    small_ref[...] = small_finish(len(rounds) - 1)
    stage_four(3)
    for index in range(chunks):
        other = total_ref.at[index, :, other_columns]
        remote(other, other, back_sems.at[0, index], back_sems.at[1, index], partner).wait_recv()

    for other in others:
        row_copy(other, me).wait_send()
    for mate in mates:
        for index in range(chunks):
            piece_copy(index, mate, line).wait_send()
            gather_copy(index, mate, line).wait_send()
    for index in range(4):
        grad_copy(index).wait_send()
    for index in range(chunks):
        half_copy(index).wait_send()
        back_copy(index).wait_send()
    for number in range(len(rounds)):
        for copy in small_copies(number, False):
            copy.wait_send()
    norm_copy.wait_send()

    @pl.when(mp == 2)
    def _():
        ext_beside.wait_send()

    @pl.when(mp == 3)
    def _():
        ext_across.wait_send()

    for copy in far_copies:
        copy.wait()


def run_backward(
    loss, x, cotangent, hidden, gain_one, gain_two, placing, d_returned, result, normed, qkv, ext,
    mixed, log_total, heads, proj, router_grad, there_in, there_out, experts,
):
    tok, width = x.shape
    rows = 2 * tok
    total = d_returned.shape[0]
    part = proj.shape[0] // 2
    lines = experts // 2
    steps = 2 if experts <= 8 else 3
    chunks = 4 if part % (16 * lines) == 0 else 2
    padded = (4 // chunks * part + 16 * lines - 1) // (16 * lines) * (16 * lines)
    small = (8 + max(8, experts), width)
    anyspace, vmem = pl.BlockSpec(memory_space=pl.ANY), pl.BlockSpec(memory_space=pltpu.VMEM)
    smem = pl.BlockSpec(memory_space=pltpu.SMEM)
    dma = pltpu.SemaphoreType.DMA
    return pl.pallas_call(
        functools.partial(backward_kernel, experts, total // experts),
        in_specs=[smem] * 4 + [vmem] * 6 + [anyspace] * 12,
        out_specs=[vmem] * 4 + [anyspace] * 2,
        out_shape=[
            jax.ShapeDtypeStruct((tok, width), bf16),
            jax.ShapeDtypeStruct((tok, width), bf16),
            jax.ShapeDtypeStruct((chunks, padded, width), bf16),
            jax.ShapeDtypeStruct(small, f32),
            jax.ShapeDtypeStruct(there_in.shape, bf16),
            jax.ShapeDtypeStruct((there_out.shape[0] // 2, width), bf16),
        ],
        scratch_shapes=[
            pltpu.VMEM(item.shape, item.dtype) for item in (mixed, proj, qkv, ext, log_total, normed, heads, x)
        ]
        + [
            pltpu.VMEM((PAIRS, HALF, 2 * PAIR), f32),
            pltpu.VMEM((PAIRS * PAIR, width), f32),
            pltpu.VMEM((total, width), bf16),
            pltpu.VMEM((tok, width), f32),
            pltpu.VMEM((rows, width), bf16),
            pltpu.VMEM((rows, PAIRS * PAIR), bf16),
            pltpu.VMEM((HALF + rows, PAIR), bf16),
            pltpu.VMEM((HALF + rows, PAIR), bf16),
            pltpu.VMEM((HALF + rows, PAIR), f32),
            pltpu.VMEM((HALF + rows, PAIR), f32),
            pltpu.VMEM((rows, 3 * PAIRS * PAIR), bf16),
            pltpu.VMEM((HALF, 2 * PAIRS * PAIR), bf16),
            pltpu.VMEM((4, part, width), f32),
            pltpu.VMEM((4 * part, width), bf16),
            pltpu.VMEM((4, part, width), bf16),
            pltpu.VMEM((tok, width), f32),
            pltpu.VMEM((tok, width), bf16),
            pltpu.VMEM((HALF, width), bf16),
            pltpu.VMEM((chunks, padded, width), bf16),
            pltpu.VMEM((chunks, padded, width // 2), bf16),
            pltpu.VMEM((chunks, lines, padded // lines, width // 2), bf16),
            pltpu.VMEM((8, width), f32),
            pltpu.VMEM((8, 8, width), f32),
            pltpu.VMEM((8, 16, width), f32),
            pltpu.VMEM((4,) + small, f32),
            dma((experts,)), dma((experts,)), dma((2,)), dma((2,)), dma((2, 2)), dma((2, 3)), dma((2, 4)),
            dma((2, chunks)), dma((2, chunks, lines)), dma((2, chunks, lines)), dma((2, chunks)),
            dma((2, steps, 8)), dma((8,)), dma((2,)),
        ],
        compiler_params=pltpu.CompilerParams(
            collective_id=2, has_side_effects=True, vmem_limit_bytes=62 * 2**20
        ),
        cost_estimate=pl.CostEstimate(flops=30 * 10**9, bytes_accessed=30 * 10**6, transcendentals=8 * 10**6),
        name="backward",
    )(
        *loss, hidden, gain_one, gain_two, placing, d_returned, router_grad,
        cotangent, result, there_in, there_out, mixed, proj, qkv, ext, log_total, normed, heads, x,
    )


def gelu_parts(pre):
    scale = 0.7978845608028654
    square = pre * pre
    inner = jnp.tanh(pre * (scale + (scale * 0.044715) * square))
    half = 0.5 * (1.0 + inner)
    slope = half + (0.5 * pre) * (1.0 - inner * inner) * (scale + (3.0 * scale * 0.044715) * square)
    return pre * half, slope

STAGES = 4

def expert_kernel(
    experts, slots, cap,
    rows_ref, cot_ref, router_ref, w_in_ref, w_out_ref, w_in_far_ref,
    back_ref, result_out, router_grad_ref, here_in_ref, here_out, there_in_ref, there_out_ref, far_grad_ref,
    result, here_out_held, router, factor, x, wi, wo, d_out, act, d_pre, total, d_x, give, g_send, g_recv,
    row_send, row_recv, back_send, back_recv, w_send, w_recv, g_send_sem, g_recv_sem, far_sems, save_sems, local_sem,
):
    me = lax.axis_index("dp")
    mp = lax.axis_index("mp")
    beside = {"mp": mp + 1 - 2 * (mp % 2)}
    across = {"mp": (mp + 2) % 4}
    members = experts // STAGES
    span = members * slots
    own_group, own_member = me // members, me % members

    def group_of(stage):
        return 2 * ((own_group // 2 + stage // 2) % 2) + (own_group % 2 + stage % 2) % 2

    def chunk(index):
        return pl.ds(pl.multiple_of(index * slots, 16), slots)

    def group_rows(group):
        return pl.ds(pl.multiple_of(group * span, 16), span)

    barrier = pltpu.get_barrier_semaphore()

    def greet(step, carry):
        pl.semaphore_signal(barrier, inc=1, device_id={"dp": (me + step) % experts}, device_id_type=MESH)
        return carry

    lax.fori_loop(1, experts, greet, 0)
    pl.semaphore_signal(barrier, inc=1, device_id=beside, device_id_type=MESH)
    pl.semaphore_signal(barrier, inc=1, device_id=across, device_id_type=MESH)
    pl.semaphore_wait(barrier, experts + 1)

    def remote(src, dst, send, recv, device):
        return pltpu.make_async_remote_copy(
            src_ref=src, dst_ref=dst, send_sem=send, recv_sem=recv, device_id=device, device_id_type=MESH
        )

    def row_copy(target, source):
        return remote(rows_ref.at[chunk(target)], x.at[chunk(source)], row_send.at[target], row_recv.at[source], {"dp": target})

    def back_copy(target, source):
        return remote(give.at[chunk(target)], back_ref.at[chunk(source)], back_send.at[target], back_recv.at[source], {"dp": target})

    def partners(stage):
        group = group_of(stage)
        if stage == 0:
            return [group * members + (own_member + k) % members for k in range(1, members)]
        return [group * members + (own_member + k) % members for k in range(members)]

    for stage in (3, 0, 1):
        for other in partners(stage):
            row_copy(other, me).start()
    own_rows = pltpu.make_async_copy(rows_ref.at[chunk(me)], x.at[chunk(me)], local_sem.at[0])
    own_in = pltpu.make_async_copy(w_in_ref, wi.at[0], local_sem.at[1])
    own_out = pltpu.make_async_copy(w_out_ref, wo.at[0], local_sem.at[2])
    far_in = pltpu.make_async_copy(w_in_far_ref, wi.at[2], local_sem.at[3])
    near_in = remote(w_in_ref, wi.at[1], w_send.at[0], w_recv.at[0], beside)
    near_out = remote(w_out_ref, wo.at[1], w_send.at[1], w_recv.at[1], beside)
    far_near_in = remote(w_in_far_ref, wi.at[3], w_send.at[2], w_recv.at[2], beside)
    far_out = remote(w_out_ref, wo.at[2], w_send.at[3], w_recv.at[3], across)
    far_near_out = remote(wo.at[2], wo.at[3], w_send.at[4], w_recv.at[4], beside)
    for copy in (own_rows, own_in, own_out, near_in, near_out, far_in, far_out, far_near_in):
        copy.start()
    router_grad_ref[...] = jnp.zeros_like(router_grad_ref)
    router[...] = router_ref[...].astype(f32)

    diagonal = lax.broadcasted_iota(jnp.int32, (slots, slots), 0) == lax.broadcasted_iota(
        jnp.int32, (slots, slots), 1
    )

    def prepare(stage, rows):
        for member in range(members):
            index = group_of(stage) * members + member
            spare = cot_ref[pl.ds(pl.multiple_of((index + 1) * slots - 16, 16), 16)].astype(f32)
            spare = spare[cap - slots + 16 : cap - slots + 17]
            value = spare[:, 0:slots] + spare[:, x.shape[1] // 2 : x.shape[1] // 2 + slots]
            factor[chunk(index)] = jnp.sum(jnp.where(diagonal, value, 0.0), axis=1, keepdims=True)
        features = x[rows].astype(f32)
        gate = jax.nn.sigmoid(jnp.sum(features * router[pl.ds(me, 1)], axis=1, keepdims=True))
        d_out[rows] = (gate * (cot_ref[rows].astype(f32) * factor[rows])).astype(bf16)
        total[rows] = jnp.zeros((span, x.shape[1]), f32)
        d_x[rows] = jnp.zeros((span, x.shape[1]), f32)

    def finish(stage, rows):
        features = x[rows].astype(f32)
        gate = jax.nn.sigmoid(jnp.sum(features * router[pl.ds(me, 1)], axis=1, keepdims=True))
        value = total[rows]
        d_gate = jnp.sum(cot_ref[rows].astype(f32) * factor[rows] * value, axis=1, keepdims=True)
        d_logit = (d_gate * gate * (1.0 - gate)).astype(bf16).astype(f32)
        give[rows] = (d_x[rows] + d_logit * router[pl.ds(me, 1)]).astype(bf16)
        result[rows] = (gate * value).astype(bf16)
        router_grad_ref[...] += jnp.sum(features * d_logit, axis=0, keepdims=True)

    def stage_of(step):
        near = jnp.where(step < 2, 0, jnp.where(step < 4, 1, 3))
        return jnp.where(step < 8, near, jnp.where(step < 12, 2, jnp.where(step < 14, 1, 0)))

    def step_body(step, carry):
        stage = stage_of(step)
        part = jnp.where(step < 6, step % 2, jnp.where((step < 8) | (step >= 12), 2 + step % 2, step - 8))
        rows = group_rows(group_of(stage))

        for static, at in enumerate((0, 2, 8, 4)):
            @pl.when(step == at)
            def _():
                if static == 0:
                    own_rows.wait()
                for other in partners(static):
                    row_copy(me, other).wait_recv()
        @pl.when((step == 0) | (step == 2) | (step == 4) | (step == 8))
        def _():
            prepare(stage, rows)

        @pl.when(step == 1)
        def _():
            for other in partners(2):
                row_copy(other, me).start()

        @pl.when(step == 0)
        def _():
            own_in.wait()
            own_out.wait()

        @pl.when(step == 1)
        def _():
            near_in.wait_recv()
            near_out.wait_recv()

        @pl.when(step == 6)
        def _():
            far_in.wait()
            far_out.wait_recv()
            far_near_out.start()

        @pl.when(step == 7)
        def _():
            far_near_in.wait_recv()
            far_near_out.wait_recv()

        pre = dot(x[rows], wi[part])
        value, slope = gelu_parts(pre)
        value = value.astype(bf16)
        act[part, rows] = value
        total[rows] += dot(value, wo[part])
        d_value = (dot(d_out[rows], wo[part], NT) * slope).astype(bf16)
        d_pre[part, rows] = d_value
        d_x[rows] += dot(d_value, wi[part], NT)

        @pl.when((step == 7) | (step == 11) | (step == 13) | (step == 15))
        def _():
            finish(stage, rows)

        for static, at in enumerate((15, 13, 11, 7)):
            @pl.when(step == at)
            def _():
                for other in partners(static):
                    back_copy(other, me).start()
        return carry

    lax.fori_loop(0, 16, step_body, 0)
    own_back = pltpu.make_async_copy(give.at[chunk(me)], back_ref.at[chunk(me)], local_sem.at[4])
    own_back.start()
    result_save = pltpu.make_async_copy(result, result_out, save_sems.at[0])
    result_save.start()

    kept = pl.ds(0, x.shape[1])
    outgoing = [g_send, act.at[3, kept], d_pre.at[3, kept], act.at[1, kept]]

    def product(left, right, store):
        def block(step, carry):
            at = pl.ds(pl.multiple_of(step * STRIP, STRIP), STRIP)
            store(at, dot(left[:, at], right[...], TN))
            return carry

        lax.fori_loop(0, x.shape[1] // STRIP, block, 0)

    def keep(target):
        def store(at, value):
            target[at] = value.astype(target.dtype)

        return store

    def grad_copy(index):
        return remote(outgoing[index], g_recv.at[index], g_send_sem.at[index], g_recv_sem.at[index], beside)

    product(act.at[3], d_out, keep(outgoing[0]))
    grad_copy(0).start()
    product(x, d_pre.at[3], keep(outgoing[1]))
    grad_copy(1).start()
    product(act.at[2], d_out, keep(total))
    product(act.at[1], d_out, keep(outgoing[2]))
    grad_copy(2).start()
    grad_copy(0).wait_recv()
    there_out_ref[...] = (total[kept] + g_recv[0].astype(f32)).astype(bf16)
    early = pl.ds(0, far_grad_ref.shape[0])
    far_grad = remote(there_out_ref.at[early], far_grad_ref, far_sems.at[0], far_sems.at[1], across)
    far_grad.start()
    product(x, d_pre.at[1], keep(outgoing[3]))
    grad_copy(3).start()
    product(x, d_pre.at[2], keep(d_x))
    product(act.at[0], d_out, keep(here_out_held))
    product(x, d_pre.at[0], keep(here_in_ref))
    grad_copy(1).wait_recv()
    there_in_ref[...] = (d_x[kept] + g_recv[1].astype(f32)).astype(bf16)
    grad_copy(2).wait_recv()
    here_out_held[...] += g_recv[2].astype(f32)
    here_save = pltpu.make_async_copy(here_out_held, here_out, save_sems.at[1])
    here_save.start()
    grad_copy(3).wait_recv()
    here_in_ref[...] += g_recv[3].astype(f32)

    result_save.wait()
    here_save.wait()
    own_back.wait()
    for stage in range(STAGES):
        for other in partners(stage):
            back_copy(me, other).wait_recv()
            back_copy(other, me).wait_send()
            row_copy(other, me).wait_send()
    for copy in (near_in, near_out, far_near_in, far_out, far_near_out):
        copy.wait_send()
    for index in range(4):
        grad_copy(index).wait_send()
    far_grad.wait()


def run_expert(rows, cot_rows, router, w_in, w_out, w_in_far, experts, cap):
    total, width = rows.shape
    slots = total // experts
    hidden = w_in.shape[1]
    anyspace, vmem = pl.BlockSpec(memory_space=pl.ANY), pl.BlockSpec(memory_space=pltpu.VMEM)
    dma = pltpu.SemaphoreType.DMA
    return pl.pallas_call(
        functools.partial(expert_kernel, experts, slots, cap),
        in_specs=[anyspace, vmem, vmem, anyspace, anyspace, anyspace],
        out_specs=[anyspace, anyspace, vmem, vmem, anyspace, vmem, vmem, anyspace],
        out_shape=[
            jax.ShapeDtypeStruct((total, width), bf16),
            jax.ShapeDtypeStruct((total, width), bf16),
            jax.ShapeDtypeStruct((1, width), f32),
            jax.ShapeDtypeStruct((width, hidden), f32),
            jax.ShapeDtypeStruct((hidden, width), f32),
            jax.ShapeDtypeStruct((width, hidden), bf16),
            jax.ShapeDtypeStruct((hidden, width), bf16),
            jax.ShapeDtypeStruct((hidden // 2, width), bf16),
        ],
        scratch_shapes=[
            pltpu.VMEM((total, width), bf16),
            pltpu.VMEM((hidden, width), f32),
            pltpu.VMEM(router.shape, f32),
            pltpu.VMEM((total, 1), f32),
            pltpu.VMEM((total, width), bf16),
            pltpu.VMEM((4, width, hidden), bf16),
            pltpu.VMEM((4, hidden, width), bf16),
            pltpu.VMEM((total, width), bf16),
            pltpu.VMEM((4, total, hidden), bf16),
            pltpu.VMEM((4, total, hidden), bf16),
            pltpu.VMEM((total, width), f32),
            pltpu.VMEM((total, width), f32),
            pltpu.VMEM((total, width), bf16),
            pltpu.VMEM((width, width), bf16),
            pltpu.VMEM((4, width, width), bf16),
            dma((experts,)), dma((experts,)), dma((experts,)), dma((experts,)),
            dma((5,)), dma((5,)), dma((4,)), dma((4,)), dma((2,)), dma((2,)), dma((5,)),
        ],
        compiler_params=pltpu.CompilerParams(
            collective_id=1, has_side_effects=True, vmem_limit_bytes=60 * 2**20
        ),
        cost_estimate=pl.CostEstimate(flops=30 * 10**9, bytes_accessed=40 * 10**6, transcendentals=3 * 10**6),
        name="expert",
    )(rows, cot_rows, router, w_in, w_out, w_in_far)


def shards(
    inputs, cotangent, routes, domains, domain_counts, domain_weights, keep_mask, gain_one, shift_one,
    w_qkv, w_proj, gain_two, shift_two, w_router, w_in, w_out,
):
    tok, width = inputs.shape
    experts = w_router.shape[1]
    cap = max(2, tok * 5 // (4 * experts))
    slots = (cap + 16) // 16 * 16
    loss = (domains, domain_counts, domain_weights, keep_mask)
    w_own = jnp.transpose(w_qkv, (1, 2, 0))
    normed, qkv, ext, mixed, log_total, heads, proj, hidden, rows, cot_rows, placing_t, w_in_far = run_forward(
        loss, inputs, cotangent, routes.reshape(1, -1), gain_one, shift_one, gain_two,
        shift_two, w_own, w_proj, w_in[0], experts, cap, slots,
    )
    d_returned, result, router_grad, here_in, here_out, there_in, there_out, far_early = run_expert(
        rows, cot_rows, w_router.T, w_in[0], w_out[0], w_in_far, experts, cap
    )
    output, input_grad, sums, small, far_in, far_out = run_backward(
        loss, inputs, cotangent, hidden, gain_one, gain_two, placing_t, d_returned, result,
        normed, qkv, ext, mixed, log_total, heads, proj, router_grad, there_in, there_out, experts,
    )
    part = w_proj.shape[0]
    sums = sums[:, : 4 * part // sums.shape[0]].reshape(4, part, -1)
    return (
        output,
        input_grad,
        small[0],
        small[1],
        jnp.transpose(sums[1:].astype(f32), (2, 0, 1)),
        sums[0].astype(f32),
        small[2],
        small[3],
        small[8 : 8 + experts].T,
        (here_in + far_in.astype(f32))[None],
        (here_out + jnp.concatenate([far_early, far_out]).astype(f32))[None],
    )


def solution(mesh):
    tokens, group = P(("dp", "mp"), None), P("dp")
    return jax.shard_map(
        shards,
        mesh=mesh,
        in_specs=(
            tokens, tokens, P("dp", None), group, P(), P(), group, P(), P(),
            P(None, None, "mp"), P("mp", None), P(), P(), P(),
            P("dp", None, "mp"), P("dp", "mp", None),
        ),
        out_specs=(
            tokens, tokens, P(), P(), P(None, None, "mp"), P("mp", None), P(), P(), P(),
            P("dp", None, "mp"), P("dp", "mp", None),
        ),
        check_vma=False,
    )
```

profile of v0, /device:TPU:12, one launch (start us, length us, event | category | flops | bytes accessed | tf_op | source)
XLA Modules:
  0.0 250.2 jit_solution(11944188414560155390)
XLA Ops:
  0.6 53.4 %forward.1 = (bf16[2048,768]{1,0:T(8,128)(2,1)}, bf16[1536,1152]{1,0:T(8,128)(2,1)}, bf16[512,768]{1,0:T(8,128)(2,1)}, bf16[1536,384]{1,0:T(8,128)(2,1)}, f32[3,...) custom-call(s32[3]{0:T(128)} %domains_ref.3, ...), custom_call_target="tpu_custom_call" | custom-call | flops 30000001024 | bytes 30000000 | tf_op jit(solution)/shard_map/forward/pallas_call | solution.py:411
  54.0 83.6 %expert.1 = (bf16[1024,768]{1,0:T(8,128)(2,1)}, bf16[1024,768]{1,0:T(8,128)(2,1)}, f32[1,768]{1,0:T(1,128)}, f32[768,768]{1,0:T(8,128)}, f32[768,768]{1,0:T(8,12...) custom-call(bf16[1024,768]{1,0:T(8,128)(2,1)} %get-tuple-element.39.rows_ref, ...), custom_call_target="tpu_custom_call" | custom-call | flops 30000001024 | bytes 40000000 | tf_op jit(solution)/shard_map/expert/pallas_call | solution.py:1231
  137.6 0.0 copy-start.3
  137.6 100.8 %backward.1 = (bf16[768,768]{1,0:T(8,128)(2,1)}, bf16[768,768]{1,0:T(8,128)(2,1)}, bf16[4,192,768]{2,1,0:T(8,128)(2,1)}, f32[16,768]{1,0:T(8,128)}, bf16[768,768]{1,0:T(8,128)(2,1)}, /*index=5*/bf16[384,768]{1,0:T(8,128)(2,1)}) custom-call(s32[3]{0:T(128)} %domains_ref.3, s32[8]{0:T(128)} %counts_ref.3, f32[8]{0:T(128)} %weights_ref.3, s32[3]{0:T(128)} %keep_ref.3, ...), custom_call_target="tpu_custom_call" | custom-call | flops 30000001024 | bytes 30000000 | tf_op jit(solution)/shard_map/backward/pallas_call | solution.py:930
  238.4 0.0 copy-done.3
  238.4 0.0 copy-start.4
  238.4 0.0 copy-start.2
  238.4 5.6 %add_bitcast_fusion = (f32[1,768,768]{2,1,0:T(8,128)}, f32[1,768,768]{2,1,0:T(8,128)}) fusion(f32[768,768]{1,0:T(8,128)} %get-tuple-element.60, bf16[384,768]{1,0:T(8,128)(2,1)} %get-tuple-element.62, bf16[384,768]{1,0:T(8,128)(2,1)S(1)} %copy-done.3, f32[768,768]{1,0:T(8,128)} %get-tuple-element.58, bf16[768,768]{1,0:T(8,128)(2,1)} %get-tuple-element.59), kind=kLoop, calls=%fused_computation | loop fusion | flops 4128768 | bytes 11796480 | tf_op jit(solution)/shard_map/broadcast_in_dim | solution.py:1306
  244.0 0.0 copy-done.4
  244.0 0.6 slice_reduce_fusion
  244.7 0.6 slice_bitcast_fusion
  245.3 0.0 copy-done.2
  245.3 0.0 copy-start.1
  245.3 0.9 bitcast_convert_fusion
  246.1 1.4 convert_bitcast_fusion
  247.5 0.0 copy-done.1
  247.5 0.0 copy-start
  247.5 1.0 copy.29
  248.5 0.7 copy-done
  249.2 1.0 copy.30
Async XLA Ops:
  137.6 100.8 %copy-start.3 = (bf16[384,768]{1,0:T(8,128)(2,1)S(1)}, bf16[384,768]{1,0:T(8,128)(2,1)}, u32[]{:S(2)}) copy-start(bf16[384,768]{1,0:T(8,128)(2,1)} %get-tuple-element.61) | copy-start | bytes 1769476
  238.4 5.6 %copy-start.4 = (f32[16,768]{1,0:T(8,128)S(1)}, f32[16,768]{1,0:T(8,128)}, u32[]{:S(2)}) copy-start(f32[16,768]{1,0:T(8,128)} %get-tuple-element.56) | copy-start | bytes 147460
  238.4 6.9 %copy-start.2 = (bf16[4,192,768]{2,1,0:T(8,128)(2,1)S(1)}, bf16[4,192,768]{2,1,0:T(8,128)(2,1)}, u32[]{:S(2)}) copy-start(bf16[4,192,768]{2,1,0:T(8,128)(2,1)} %get-tuple-element.57) | copy-start | bytes 3538948
  245.3 2.2 copy-start.1
  247.5 1.7 copy-start
where the time goes:
time: 252 us; the launch traced here: 250 us
  Pallas kernels  238 us (94%)
  other arithmetic  7.8 us (3%)
  local copies, waits for them, and re-layouts  3.96 us (2%)
    pallas_call x1, Pallas kernels, run_backward(): pl.pallas_call(functools.partial(backward_kernel, experts, total // exper...  101 us
    pallas_call x1, Pallas kernels, run_expert(): pl.pallas_call(functools.partial(expert_kernel, experts, slots, cap), in_...  83.6 us
    pallas_call x1, Pallas kernels, run_forward(): pl.pallas_call(functools.partial(forward_kernel, experts, slots, cap), in...  53.4 us
    broadcast_in_dim x1, other arithmetic, shards(): (here_out + jnp.concatenate([far_early, far_out]).astype(f32))[None]  5.6 us

commit v1 on v0

--- a/solution.py
+++ b/solution.py
@@ -781,7 +781,6 @@
     norm_copy.start()
     lax.fori_loop(0, tok // STRIP, pull_norm, 0)
     stage_two(0)
-    stage_one(1)
     own_rows.wait()
     for other in others:
         row_copy(me, other).wait_recv()
@@ -793,8 +792,7 @@
 
     lax.fori_loop(0, tok // STRIP, finish, 0)
     stage_three(0)
-    stage_two(1)
-    stage_one(2)
+    stage_one(1)
     norm_copy.wait_recv()
     loads[7].wait()
 
@@ -815,6 +813,8 @@
         return carry
 
     lax.fori_loop(0, tok // STRIP, first_norm, 0)
+    stage_two(1)
+    stage_one(2)
 
     small[4:5] = router_ref[...]
     rounds = [(first_slots, "dp", me, me - me % 8, 1, 8)]
@@ -1183,16 +1183,16 @@
 
     product(act.at[3], d_out, keep(outgoing[0]))
     grad_copy(0).start()
+    product(act.at[2], d_out, keep(total))
     product(x, d_pre.at[3], keep(outgoing[1]))
     grad_copy(1).start()
-    product(act.at[2], d_out, keep(total))
-    product(act.at[1], d_out, keep(outgoing[2]))
-    grad_copy(2).start()
     grad_copy(0).wait_recv()
     there_out_ref[...] = (total[kept] + g_recv[0].astype(f32)).astype(bf16)
     early = pl.ds(0, far_grad_ref.shape[0])
     far_grad = remote(there_out_ref.at[early], far_grad_ref, far_sems.at[0], far_sems.at[1], across)
     far_grad.start()
+    product(act.at[1], d_out, keep(outgoing[2]))
+    grad_copy(2).start()
     product(x, d_pre.at[1], keep(outgoing[3]))
     grad_copy(3).start()
     product(x, d_pre.at[2], keep(d_x))

time: 252 us -> 251 us (level)
  no operation moved by 1% of the time
where the time goes in v1:
time: 251 us; the launch traced here: 250 us
  Pallas kernels  238 us (95%)
  other arithmetic  7.8 us (3%)
  local copies, waits for them, and re-layouts  3.96 us (2%)
    pallas_call x1, Pallas kernels, run_backward(): pl.pallas_call(functools.partial(backward_kernel, experts, total // exper...  103 us
    pallas_call x1, Pallas kernels, run_expert(): pl.pallas_call(functools.partial(expert_kernel, experts, slots, cap), in_...  81.6 us
    pallas_call x1, Pallas kernels, run_forward(): pl.pallas_call(functools.partial(forward_kernel, experts, slots, cap), in...  53.4 us
    broadcast_in_dim x1, other arithmetic, shards(): (here_out + jnp.concatenate([far_early, far_out]).astype(f32))[None]  5.6 us

profile of v1, /device:TPU:12, one launch (start us, length us, event | category | flops | bytes accessed | tf_op | source)
XLA Modules:
  0.0 250.5 jit_solution(15267028068023260875)
XLA Ops:
  0.6 53.4 %forward.1 = (bf16[2048,768]{1,0:T(8,128)(2,1)}, bf16[1536,1152]{1,0:T(8,128)(2,1)}, bf16[512,768]{1,0:T(8,128)(2,1)}, bf16[1536,384]{1,0:T(8,128)(2,1)}, f32[3,...) custom-call(s32[3]{0:T(128)} %domains_ref.3, ...), custom_call_target="tpu_custom_call" | custom-call | flops 30000001024 | bytes 30000000 | tf_op jit(solution)/shard_map/forward/pallas_call | solution.py:411
  54.0 81.6 %expert.1 = (bf16[1024,768]{1,0:T(8,128)(2,1)}, bf16[1024,768]{1,0:T(8,128)(2,1)}, f32[1,768]{1,0:T(1,128)}, f32[768,768]{1,0:T(8,128)}, f32[768,768]{1,0:T(8,12...) custom-call(bf16[1024,768]{1,0:T(8,128)(2,1)} %get-tuple-element.39.rows_ref, ...), custom_call_target="tpu_custom_call" | custom-call | flops 30000001024 | bytes 40000000 | tf_op jit(solution)/shard_map/expert/pallas_call | solution.py:1231
  135.7 0.0 copy-start.3
  135.7 102.9 %backward.1 = (bf16[768,768]{1,0:T(8,128)(2,1)}, bf16[768,768]{1,0:T(8,128)(2,1)}, bf16[4,192,768]{2,1,0:T(8,128)(2,1)}, f32[16,768]{1,0:T(8,128)}, bf16[768,768]{1,0:T(8,128)(2,1)}, /*index=5*/bf16[384,768]{1,0:T(8,128)(2,1)}) custom-call(s32[3]{0:T(128)} %domains_ref.3, s32[8]{0:T(128)} %counts_ref.3, f32[8]{0:T(128)} %weights_ref.3, s32[3]{0:T(128)} %keep_ref.3, ...), custom_call_target="tpu_custom_call" | custom-call | flops 30000001024 | bytes 30000000 | tf_op jit(solution)/shard_map/backward/pallas_call | solution.py:930
  238.7 0.0 copy-done.3
  238.7 0.0 copy-start.4
  238.7 0.0 copy-start.2
  238.7 5.6 %add_bitcast_fusion = (f32[1,768,768]{2,1,0:T(8,128)}, f32[1,768,768]{2,1,0:T(8,128)}) fusion(f32[768,768]{1,0:T(8,128)} %get-tuple-element.60, bf16[384,768]{1,0:T(8,128)(2,1)} %get-tuple-element.62, bf16[384,768]{1,0:T(8,128)(2,1)S(1)} %copy-done.3, f32[768,768]{1,0:T(8,128)} %get-tuple-element.58, bf16[768,768]{1,0:T(8,128)(2,1)} %get-tuple-element.59), kind=kLoop, calls=%fused_computation | loop fusion | flops 4128768 | bytes 11796480 | tf_op jit(solution)/shard_map/broadcast_in_dim | solution.py:1306
  244.3 0.0 copy-done.4
  244.3 0.6 slice_reduce_fusion
  244.9 0.6 slice_bitcast_fusion
  245.5 0.0 copy-done.2
  245.5 0.0 copy-start.1
  245.5 0.9 bitcast_convert_fusion
  246.4 1.4 convert_bitcast_fusion
  247.7 0.0 copy-done.1
  247.7 0.0 copy-start
  247.7 1.0 copy.29
  248.8 0.7 copy-done
  249.4 1.0 copy.30
Async XLA Ops:
  135.7 103.0 %copy-start.3 = (bf16[384,768]{1,0:T(8,128)(2,1)S(1)}, bf16[384,768]{1,0:T(8,128)(2,1)}, u32[]{:S(2)}) copy-start(bf16[384,768]{1,0:T(8,128)(2,1)} %get-tuple-element.61) | copy-start | bytes 1769476
  238.7 5.6 %copy-start.4 = (f32[16,768]{1,0:T(8,128)S(1)}, f32[16,768]{1,0:T(8,128)}, u32[]{:S(2)}) copy-start(f32[16,768]{1,0:T(8,128)} %get-tuple-element.56) | copy-start | bytes 147460
  238.7 6.9 %copy-start.2 = (bf16[4,192,768]{2,1,0:T(8,128)(2,1)S(1)}, bf16[4,192,768]{2,1,0:T(8,128)(2,1)}, u32[]{:S(2)}) copy-start(bf16[4,192,768]{2,1,0:T(8,128)(2,1)} %get-tuple-element.57) | copy-start | bytes 3538948
  245.5 2.2 copy-start.1
  247.7 1.7 copy-start
